TPU v7x, 512 devices: a whole 4x4x16 slice. The times are simulated.
512 devices in a mesh: chan: 128 (over x, z, core), tm: 4 (over y).
Axes of the slice: x: 4, y: 4, z: 16, core: 2. Of those that a mesh axis runs over, the one named last changes fastest.
Arguments:
- voltages: bfloat16 [2, 1024, 262144], P(None, 'chan', 'tm'), may hold values from -6 to 6
- flags: int32 [512, 64], P('chan', 'tm'), may hold values 0 or 1
- pairs: int32 [2, 2], replicated, may hold values from 0 to 15
Outputs:
- visibilities: float32 [4096, 2, 64, 128], P(('chan', 'tm'))
All inputs are finite; a program needn't handle non-finite values. No bound on the sum of `flags` on one device may be relied on, other than what follows from the above.
Results may differ from a plain program's by a relative error of at most 0.0082.
Values may be sent and summed in bfloat16 or wider, within the bound.
A program may use at most 128 MiB of HBM per device.

v0:
```python
import math

import jax
import jax.numpy as jnp
from jax import lax
from jax.sharding import PartitionSpec as P

CHANNELS = 4096
TAPS = 16
BLOCK = 64


def shifted(x, axis, by):
    length = lax.axis_size(axis)
    pairs = [(i, i + by) for i in range(length) if 0 <= i + by < length]
    return lax.ppermute(x, axis, pairs)


def window_table():
    length = TAPS * CHANNELS
    index = jnp.arange(length).astype(jnp.float32)
    offset = (index - length / 2 + 0.5) / CHANNELS
    taper = 0.5 - 0.5 * jnp.cos(2.0 * math.pi * (index + 0.5) / length)
    return (jnp.sinc(offset) * taper).reshape(TAPS, CHANNELS)


def dft_table(order, factor):
    counts = jnp.arange(order)
    angle = (counts[:, None] * counts[None, :] % order).astype(jnp.float32) * (
        2.0 * math.pi / order
    )
    cosine = jnp.cos(angle) * factor
    sine = jnp.sin(angle) * factor
    upper = jnp.stack([cosine, -sine], axis=1)
    lower = jnp.stack([sine, cosine], axis=1)
    return jnp.stack([upper, lower], axis=0)


def analyse(extended, live_mask):
    frames = extended.shape[2] - (TAPS - 1)
    inner = CHANNELS // 16
    window = window_table()
    total = jnp.zeros((2, extended.shape[1], frames, CHANNELS), jnp.float32)
    for step in range(TAPS):
        total = total + window[step] * extended[:, :, step : step + frames, :]
    filtered = total.astype(jnp.bfloat16)
    pieces = filtered.reshape(2, extended.shape[1], frames, 16, inner)
    first = dft_table(16, 0.25).astype(jnp.bfloat16)
    partial_value = jnp.einsum(
        "rgfnq,rnsk->gfksq", pieces, first, preferred_element_type=jnp.float32
    )
    coarse = jnp.arange(16)
    fine_idx = jnp.arange(inner)
    angle = (coarse[:, None] * fine_idx[None, :]).astype(jnp.float32) * (2.0 * math.pi / CHANNELS)
    cosine = jnp.cos(angle)
    sine = jnp.sin(angle)
    real_part = partial_value[:, :, :, 0, :]
    imag_part = partial_value[:, :, :, 1, :]
    rot_real = real_part * cosine + imag_part * sine
    rot_imag = imag_part * cosine - real_part * sine
    rotated = jnp.stack([rot_real, rot_imag], axis=3).astype(jnp.bfloat16)
    rotated = rotated.reshape(extended.shape[1], frames, 16, 2 * inner)
    second = (
        dft_table(inner, 1.0 / math.sqrt(inner)).astype(jnp.bfloat16).reshape(2 * inner, 2, inner)
    )
    spectrum = jnp.einsum("gfkn,nrq->qkrfg", rotated, second, preferred_element_type=jnp.float32)
    spectrum = spectrum * jnp.transpose(live_mask)
    return spectrum.astype(jnp.bfloat16).reshape(CHANNELS, 2, frames, extended.shape[1])


def cross_blocks(turned, pairs, norm_scale):
    count = turned.shape[0]
    rows_all = 2 * turned.shape[2]

    def one_pair(block_pair):
        left_block = lax.dynamic_slice_in_dim(turned, block_pair[0] * BLOCK, BLOCK, 3)
        right_block = lax.dynamic_slice_in_dim(turned, block_pair[1] * BLOCK, BLOCK, 3)
        a_side = left_block.reshape(count, rows_all, BLOCK)
        b_real = right_block.reshape(count, rows_all, BLOCK)
        b_imag = jnp.concatenate([-right_block[:, 1], right_block[:, 0]], axis=1)
        b_side = jnp.concatenate([b_real, b_imag], axis=2)
        return (
            jnp.einsum("cxi,cxj->cij", a_side, b_side, preferred_element_type=jnp.float32)
            * norm_scale
        )

    result = lax.map(one_pair, pairs)
    return jnp.transpose(result, (1, 0, 2, 3))


def local(voltages, flags, pairs):
    group_size = voltages.shape[1]
    frames = voltages.shape[2] // CHANNELS
    framed = voltages.reshape(2, group_size, frames, CHANNELS)
    time_count = lax.axis_size("tm")
    norm_scale = 1.0 / (frames * time_count)
    before = shifted(framed[:, :, frames - (TAPS - 1) :, :], "tm", 1)
    extended = jnp.concatenate([before, framed], axis=2)
    live_mask = jnp.repeat(flags, 2, axis=0).astype(jnp.float32)
    spectra = analyse(extended, live_mask)
    turned = lax.all_to_all(spectra, "chan", split_axis=0, concat_axis=3, tiled=True)
    partial_value = cross_blocks(turned, pairs, norm_scale)
    return lax.psum_scatter(partial_value, "tm", scatter_dimension=0, tiled=True)


def solution(mesh):
    placed = (P(None, "chan", "tm"), P("chan", "tm"), P())
    return jax.shard_map(
        local,
        mesh=mesh,
        in_specs=placed,
        out_specs=P(("chan", "tm"), None, None, None),
        check_vma=False,
    )
```

profile of v0, /device:TPU:1, one launch (start us, length us, event | category | flops | bytes accessed | tf_op | source)
XLA Modules:
  0.0 324.5 jit_solution(16400642373485783403)
XLA Ops:
  6.5 1.8 slice.167
  8.4 4.2 %collective-permute-start = (bf16[2,8,15,4096]{3,1,2,0:T(8,128)(2,1)S(1)}, bf16[2,8,15,4096]{3,1,2,0:T(8,128)(2,1)S(1)}, u32[]{:S(2)}, u32[]{:S(2)}) collective-permute-start(bf16[2,8,15,4096]{3,1,2,0:T(8,128)(2,1)S(1)} %slice.167), channel_id=1, source_target_pairs={{0,1},{1,2},{2,3},{4,5},{5,6},{6,7},{8,9},{9,10},{10,11},{12,13},{... | collective-permute-start | bytes 5898248 | tf_op jit(solution)/shard_map/ppermute | solution.py:16
  12.6 0.1 fusion.60
  12.6 0.1 negate_convert_fusion.1
  12.7 0.1 fusion.52
  12.8 1.0 fusion.49
  13.8 1.1 negate_convert_fusion
  14.9 1.2 fusion.34
  16.2 34.5 %collective-permute-done = bf16[2,8,15,4096]{3,1,2,0:T(8,128)(2,1)S(1)} collective-permute-done((bf16[2,8,15,4096]{3,1,2,0:T(8,128)(2,1)S(1)}, bf16[2,8,15,4096]{3,1,2,0:T(8,128)(2,1)S(1)}, u32[]{:S(2)}, u32[]{:S(2)}) %collective-permute-start) | collective-permute-done | bytes 1966112 | tf_op jit(solution)/shard_map/ppermute | solution.py:16
  50.6 9.2 %add_convert_fusion = bf16[2,8,16,4096]{3,1,2,0:T(8,128)(2,1)S(1)} fusion(bf16[2,8,16,4096]{3,1,2,0:T(8,128)(2,1)S(1)} %bitcast.97, bf16[2,8,15,4096]{3,1,2,0:T(8,128)(2,1)S(1)} %collective-permute-done, f32[4096]{0:T(1024)S(1)} %get-tuple-element.57, f32[4096]{0:T(1024)S(1)} %get-tuple-element.58, f32[4096]{0:T(1024)S(1)} %get-tuple-element.59, ...), kind=kLoop, calls=%fused_computation.45 | loop fusion | flops 66060288 | bytes 6422528 | tf_op jit(solution)/shard_map/convert_element_type | solution.py:46
  59.8 0.6 copy.55
  60.5 0.8 convolution_bitcast_fusion
  61.2 0.7 add_convert_fusion.1
  62.0 1.3 fusion.9
  63.3 24.3 %copy.49 = bf16[256,16,2,16,8]{3,4,2,1,0:T(8,128)(2,1)} copy(bf16[256,16,2,16,8]{0,1,3,4,2:T(8,128)(2,1)S(1)} %fusion.9) | data formatting | bytes 4194304 | tf_op jit(solution)/shard_map/reshape | solution.py:68
  87.6 23.2 %reshape.275 = bf16[128,2,4096]{2,1,0:T(2,128)(2,1)} reshape(bf16[4096,2,8,16]{3,2,1,0:T(8,128)(2,1)} %bitcast.89) | data formatting | bytes 4194304
  110.8 23.8 %all-to-all-start = ((bf16[128,2,4096]{2,1,0:T(2,128)(2,1)}), bf16[128,2,4096]{2,1,0:T(2,128)(2,1)S(1)}, u32[]{:S(2)}, u32[]{:S(2)}) async-start(bf16[128,2,4096]{2,1,0:T(2,128)(2,1)} %reshape.275), calls=%async_computation | async-start | bytes 4194304 | tf_op jit(solution)/shard_map/all_to_all | solution.py:101
  134.7 0.0 reduce-scatter.2.cloned.1.call-start
  134.7 99.1 %all-to-all-done = bf16[128,2,4096]{2,1,0:T(2,128)(2,1)S(1)} async-done(((bf16[128,2,4096]{2,1,0:T(2,128)(2,1)}), bf16[128,2,4096]{2,1,0:T(2,128)(2,1)S(1)}, u32[]{:S(2)}, u32[]{:S(2)}) %all-to-all-start) | async-done | bytes 2097184 | tf_op jit(solution)/shard_map/all_to_all | solution.py:101
  233.8 14.3 %reshape.276 = bf16[4096,2,8,16]{3,2,1,0:T(8,128)(2,1)} reshape(bf16[128,2,4096]{2,1,0:T(2,128)(2,1)S(1)} %all-to-all-done) | data formatting | bytes 4194304
  248.1 22.1 %copy.41 = bf16[32,2,16,128,8]{0,4,3,2,1:T(8,128)(2,1)} copy(bf16[32,2,16,128,8]{2,4,1,0,3:T(8,128)(2,1)} %bitcast.90) | data formatting | bytes 4194304 | tf_op jit(solution)/shard_map/all_to_all | solution.py:101
  270.2 7.5 %copy.42 = bf16[32,2,16,1024]{3,2,0,1:T(8,128)(2,1)S(1)} copy(bf16[32,2,16,1024]{0,3,2,1:T(8,128)(2,1)} %bitcast.91) | data formatting | bytes 4194304 | tf_op jit(solution)/shard_map/while | solution.py:87
  277.7 7.7 %while.10 = (s32[]{:T(128)}, f32[2,32,64,128]{3,2,0,1:T(8,128)}, s32[2,2]{1,0:T(2,128)S(1)}, bf16[32,2,16,1024]{3,2,0,1:T(8,128)(2,1)S(1)}, s32[]{:T(128)}, /*index=5*/s32[1,1]{1,0:T(1,128)}, s32[]{:T(128)}, s32[]{:T(128)}, s32[]{}) while((s32[]{:T(128)}, f32[2,32,64,128]{3,2,0,1:T(8,128)}, s32[2,2]{1,0:T(2,128)S(1)}, ...), condition=%wide.region_1.2_spmd, body=%wide.region_0.1_spmd.sunk | while | flops 17924108 | bytes 2753273 | solution.py:87
  277.8 0.7 fusion.73
  279.7 0.2 constant_dynamic-slice_fusion.6
  280.0 0.1 fusion.74
  280.1 1.5 fusion.75
  281.6 0.7 fusion.73
  283.5 0.2 constant_dynamic-slice_fusion.6
  283.8 0.1 fusion.74
  284.0 1.5 fusion.75
  285.5 32.1 %reduce-scatter.2.cloned.1.call-done = f32[8,2,64,128]{3,2,1,0:T(8,128)} async-done(((f32[32,2,64,128]{3,2,1,0:T(8,128)}), f32[8,2,64,128]{3,2,1,0:T(8,128)}) %reduce-scatter.2.cloned.1.call-update) | async-done | bytes 524304 | tf_op jit(solution)/shard_map/reduce_scatter | solution.py:103
  (19 shorter events, 0.2 us)
Async XLA Ops:
  6.5 6.0 %copy-start.1 = (s32[4,16]{1,0:T(4,128)S(1)}, s32[4,16]{1,0:T(4,128)}, u32[]{:S(2)}) copy-start(s32[4,16]{1,0:T(4,128)} %param.6) | copy-start | bytes 772
  6.5 44.1 %copy-start = (bf16[2,8,65536]{2,1,0:T(8,128)(2,1)S(1)}, bf16[2,8,65536]{2,1,0:T(8,128)(2,1)}, u32[]{:S(2)}) copy-start(bf16[2,8,65536]{2,1,0:T(8,128)(2,1)} %param.5) | copy-start | bytes 6291460
  8.4 42.3 %collective-permute-start = (bf16[2,8,15,4096]{3,1,2,0:T(8,128)(2,1)S(1)}, bf16[2,8,15,4096]{3,1,2,0:T(8,128)(2,1)S(1)}, u32[]{:S(2)}, u32[]{:S(2)}) collective-permute-start(bf16[2,8,15,4096]{3,1,2,0:T(8,128)(2,1)S(1)} %slice.167), channel_id=1, source_target_pairs={{0,1},{1,2},{2,3},{4,5},{5,6},{6,7},{8,9},{9,10},{10,11},{12,13},{... | collective-permute-start | bytes 5898248 | tf_op jit(solution)/shard_map/ppermute | solution.py:16
  110.8 123.0 %all-to-all-start = ((bf16[128,2,4096]{2,1,0:T(2,128)(2,1)}), bf16[128,2,4096]{2,1,0:T(2,128)(2,1)S(1)}, u32[]{:S(2)}, u32[]{:S(2)}) async-start(bf16[128,2,4096]{2,1,0:T(2,128)(2,1)} %reshape.275), calls=%async_computation | async-start | bytes 4194304 | tf_op jit(solution)/shard_map/all_to_all | solution.py:101
  134.7 182.9 %reduce-scatter.2.cloned.1.call-start = ((), (), s32[]{:S(2)}) async-start(), calls=%async_computation.2 | async-start | bytes 2621440 | tf_op jit(solution)/shard_map/reduce_scatter | solution.py:103
  270.2 7.5 %copy-start.2 = (s32[2,2]{1,0:T(2,128)S(1)}, s32[2,2]{1,0:T(2,128)}, u32[]{:S(2)}) copy-start(s32[2,2]{1,0:T(2,128)} %param.7) | copy-start | bytes 52
Sparse Core Ops, SparseCore 0:
  285.6 31.9 reduce-scatter.1
where the time goes:
time: 326 us; the launch traced here: 324 us
  waiting for transfers between devices  166 us (51%)
  local copies, waits for them, and re-layouts  95.8 us (29%)
  starting transfers between devices  28 us (9%)
  other arithmetic  13.8 us (4%)
  between operations  13.6 us (4%)
  matrix products  4.99 us (2%)
    all_to_all x1, waiting for transfers between devices, local(): lax.all_to_all(spectra, 'chan', split_axis=0, concat_axis=3, tiled=True)  99.1 us
    unnamed x9, local copies, waits for them, and re-layouts  38.2 us
    ppermute x1, waiting for transfers between devices, shifted(): return lax.ppermute(x, axis, pairs)  34.5 us
    reduce_scatter x1, waiting for transfers between devices, local(): lax.psum_scatter(partial_value, 'tm', scatter_dimension=0, tiled=True)  32.1 us
    reshape x1, local copies, waits for them, and re-layouts, analyse(): spectrum.astype(jnp.bfloat16)  24.3 us
    all_to_all x1, starting transfers between devices, local(): lax.all_to_all(spectra, 'chan', split_axis=0, concat_axis=3, tiled=True)  23.8 us
    all_to_all x1, local copies, waits for them, and re-layouts, local(): lax.all_to_all(spectra, 'chan', split_axis=0, concat_axis=3, tiled=True)  22.1 us
    convert_element_type x1, other arithmetic, analyse(): filtered = total.astype(jnp.bfloat16)  9.18 us
  transfers between devices with their start and end apart: 3, of which 3 were waited for; matrix products, arithmetic and copies ran while one was open for 1% of the time, Pallas kernels for 0%

commit v1 on v0

v1 whole, which is shorter than its diff:
```python
import functools
import math

import jax
import jax.numpy as jnp
import ml_dtypes
import numpy as np
from jax import lax
from jax.experimental import pallas as pl
from jax.experimental.pallas import tpu as pltpu
from jax.sharding import PartitionSpec as P

CHANNELS = 4096
TAPS = 16
BLOCK = 64
NX, NZ, NC, NY = 4, 16, 2, 4
LOCAL = 16
FRAMES = 64
INNER = 256
MESH = pl.DeviceIdType.MESH


def window_table():
    length = TAPS * CHANNELS
    index = np.arange(length, dtype=np.float64)
    offset = (index - length / 2 + 0.5) / CHANNELS
    taper = 0.5 - 0.5 * np.cos(2.0 * math.pi * (index + 0.5) / length)
    return (np.sinc(offset) * taper).astype(np.float32).reshape(TAPS, 16, INNER)


def dft_table(order, factor):
    counts = np.arange(order)
    angle = (counts[:, None] * counts[None, :] % order).astype(np.float64) * (2.0 * math.pi / order)
    cosine = np.cos(angle) * factor
    sine = np.sin(angle) * factor
    upper = np.stack([cosine, -sine], axis=1)
    lower = np.stack([sine, cosine], axis=1)
    table = np.stack([upper, lower], axis=0)
    return table.astype(np.float32).astype(ml_dtypes.bfloat16)


def first_table():
    first = dft_table(16, 0.25).astype(np.float32)
    table = np.zeros((2, 16, 8, 8, 2, 16), np.float32)
    for f in range(8):
        table[:, :, f, f] = first.transpose(2, 3, 0, 1)
    return table.reshape(256, 256).astype(ml_dtypes.bfloat16)


def twiddle_tables():
    angle = np.arange(16)[:, None] * np.arange(INNER)[None, :] * (2.0 * math.pi / CHANNELS)
    angle = np.repeat(angle, 8, axis=0)
    return np.cos(angle).astype(np.float32), np.sin(angle).astype(np.float32)


def second_table():
    second = dft_table(INNER, 1.0 / math.sqrt(INNER))
    second = second.transpose(3, 2, 0, 1).reshape(NX, NZ, NC, 2, 2, 2 * INNER)
    return np.ascontiguousarray(second.transpose(0, 2, 3, 4, 1, 5)).reshape(2 * INNER, 2 * INNER)


def place():
    chan = lax.axis_index("chan")
    return (
        lax.div(chan, NZ * NC),
        lax.rem(lax.div(chan, NC), NZ),
        lax.rem(chan, NC),
        lax.axis_index("tm"),
    )


def device(x, z, c, y):
    return ((x * NZ + z) * NC + c, y)


def plan_kernel(pairs_ref, plan_ref):
    zero, one = jnp.int32(0), jnp.int32(1)
    block = [pairs_ref[s // 2, s % 2] for s in range(4)]
    across = [lax.div(b, 4) for b in block]
    quarter = [lax.rem(b, 4) for b in block]
    fresh, order = [], []
    for s in range(4):
        new, spot = one, zero
        for e in range(s):
            spot = spot + jnp.where(quarter[e] == quarter[s], fresh[e], zero)
        for e in range(s):
            same = block[e] == block[s]
            spot = jnp.where(same, order[e], spot)
            new = jnp.where(same, zero, new)
        fresh.append(new)
        order.append(spot)
    most = zero
    for q in range(4):
        count = zero
        for s in range(4):
            count = count + jnp.where(quarter[s] == q, fresh[s], zero)
        most = jnp.maximum(most, count)
        for m in range(4):
            pick = zero
            for s in range(4):
                hit = (quarter[s] == q) & (order[s] == m)
                pick = jnp.where(hit, across[s], pick)
            plan_ref[4 * q + m] = pick
    for s in range(4):
        plan_ref[16 + s] = quarter[s]
        plan_ref[20 + s] = order[s]
    plan_ref[24] = most - 1


def front_kernel(
    volts, flags, window, first, cosine, sine, second,
    turned,
    line, marks, filtered, spectra,
    y_send, y_recv, f_send, f_recv, x_send, x_recv, own,
):
    x, z, c, y = place()
    barrier = pltpu.get_barrier_semaphore()
    y_peers = [(d, lax.rem(y + d, NY)) for d in (1, 3, 2)]
    x_peers = [
        (2 * dx + dc, lax.rem(x + dx, NX), lax.rem(c + dc, NC))
        for dx in (2, 1, 3, 0)
        for dc in (0, 1)
        if dx + dc > 0
    ]
    for _, other in y_peers:
        pl.semaphore_signal(barrier, inc=1, device_id=device(x, z, c, other), device_id_type=MESH)
    for _, ox, oc in x_peers:
        pl.semaphore_signal(barrier, inc=1, device_id=device(ox, z, oc, y), device_id_type=MESH)
    pl.semaphore_wait(barrier, len(y_peers) + len(x_peers))

    here = pl.ds(LOCAL + LOCAL * y, LOCAL)
    incoming = [[], []]
    for d, other in y_peers:
        copy = pltpu.make_async_remote_copy(
            src_ref=flags.at[other], dst_ref=marks.at[y],
            send_sem=f_send.at[d - 1], recv_sem=f_recv.at[d - 1],
            device_id=device(x, z, c, other), device_id_type=MESH,
        )
        copy.start()
        incoming[0].append(copy)
    mine = pltpu.make_async_copy(flags.at[y], marks.at[y], own.at[4])
    mine.start()
    kept = [[mine], []]
    for j in range(2):
        for d, other in y_peers:
            copy = pltpu.make_async_remote_copy(
                src_ref=volts.at[2 * other + j], dst_ref=line.at[j, :, here],
                send_sem=y_send.at[j, d - 1], recv_sem=y_recv.at[j, d - 1],
                device_id=device(x, z, c, other), device_id_type=MESH,
            )
            copy.start()
            incoming[j].append(copy)
        mine = pltpu.make_async_copy(volts.at[2 * y + j], line.at[j, :, here], own.at[j])
        mine.start()
        kept[j].append(mine)

    line[:, :, 0:LOCAL] = jnp.zeros((2, 2, LOCAL, 16, INNER), jnp.bfloat16)

    outgoing = []
    for j in range(2):
        for copy in incoming[j]:
            copy.wait_recv()
        for copy in kept[j]:
            copy.wait()

        for half in range(2):
            lanes = slice(128 * half, 128 * half + 128)

            def sift(step, _, j=j, lanes=lanes):
                p = lax.div(step, 8)
                base = lax.rem(step, 8) * 8
                taps = [window[t, :, lanes] for t in range(TAPS)]
                total = [None] * 8
                for u in range(8 + TAPS - 1):
                    value = line[j, p, base + 1 + u, :, lanes].astype(jnp.float32)
                    for g in range(8):
                        t = u - g
                        if 0 <= t < TAPS:
                            term = taps[t] * value
                            total[g] = term if t == 0 else total[g] + term
                for g in range(8):
                    filtered[base + g, p, :, lanes] = total[g].astype(jnp.bfloat16)
                return 0

            lax.fori_loop(0, 16, sift, 0)

        def transform(part, _, j=j):
            reals, imags = [], []
            for half in range(2):
                block = filtered[pl.ds(part * LOCAL + 8 * half, 8)].reshape(256, INNER)
                value = jnp.dot(first[...], block, preferred_element_type=jnp.float32)
                real, imag = value[:128], value[128:]
                rot_real = real * cosine[...] + imag * sine[...]
                rot_imag = imag * cosine[...] - real * sine[...]
                reals.append(rot_real.reshape(16, 8, INNER))
                imags.append(rot_imag.reshape(16, 8, INNER))
            real = jnp.concatenate(reals, axis=1).reshape(256, INNER)
            imag = jnp.concatenate(imags, axis=1).reshape(256, INNER)
            rotated = jnp.concatenate([real, imag], axis=1).astype(jnp.bfloat16)
            out = lax.dot_general(
                second[...], rotated, (((1,), (1,)), ((), ())), preferred_element_type=jnp.float32
            )
            live = marks[part][0:1].astype(jnp.float32)
            out = out * jnp.concatenate([live, live], axis=1)
            out = out.astype(jnp.bfloat16).reshape(NX, NC, 2, 2, NZ, 256)
            for yy in range(NY):
                low = 128 * (yy % 2)
                spectra[j, :, :, yy, part] = out[:, :, yy // 2, :, :, low : low + 128]
            return 0

        lax.fori_loop(0, 4, transform, 0)

        for k, ox, oc in x_peers:
            copy = pltpu.make_async_remote_copy(
                src_ref=spectra.at[j, ox, oc], dst_ref=turned.at[j, x, c],
                send_sem=x_send.at[j, k - 1], recv_sem=x_recv.at[j, k - 1],
                device_id=device(ox, z, oc, y), device_id_type=MESH,
            )
            copy.start()
            outgoing.append(copy)
        mine = pltpu.make_async_copy(spectra.at[j, x, c], turned.at[j, x, c], own.at[2 + j])
        mine.start()
        kept[j] = [mine]

    for copies in incoming:
        for copy in copies:
            copy.wait_send()
    for copy in outgoing:
        copy.wait_recv()
        copy.wait_send()
    for j in range(2):
        kept[j][0].wait()


def back_kernel(count, plan, turned, result, board, ready, landed, send_sem, recv_sem):
    x, z, c, y = place()
    zh, zl = lax.div(z, 4), lax.rem(z, 4)
    barrier = pltpu.get_barrier_semaphore()
    peers = NZ * NY

    def partner(step):
        return lax.rem(z + lax.div(step, NY), NZ), lax.rem(y + lax.rem(step, NY), NY)

    def greet(step, _):
        oz, oy = partner(step)
        pl.semaphore_signal(barrier, inc=1, device_id=device(x, oz, c, oy), device_id_type=MESH)
        return 0

    lax.fori_loop(1, peers, greet, 0)

    for m in range(count):
        which = plan[zh * 4 + m]

        def regroup(step, _, m=m, which=which):
            core, yy = lax.div(step, NY), lax.rem(step, NY)
            for j in range(2):
                piece = turned[j, which, core, yy].astype(jnp.float32)
                board[pl.ds(128 * j, 128), :] = piece.reshape(128, 128)
            for oz in range(NZ):
                rows = board[pl.ds(oz, 16, stride=16), :]
                ready[oz * NY + yy, m, core] = rows.astype(jnp.bfloat16)
            return 0

        lax.fori_loop(0, NC * NY, regroup, 0)

    pl.semaphore_wait(barrier, peers - 1)

    def send(step, _):
        oz, oy = partner(step)
        pltpu.make_async_remote_copy(
            src_ref=ready.at[oz * NY + oy], dst_ref=landed.at[zh, zl, :, :, y],
            send_sem=send_sem, recv_sem=recv_sem,
            device_id=device(x, oz, c, oy), device_id_type=MESH,
        ).start()
        return 0

    lax.fori_loop(1, peers, send, 0)
    pltpu.make_async_copy(ready.at[z * NY + y], landed.at[zh, zl, :, :, y], recv_sem).start()
    pltpu.make_async_copy(landed, landed, recv_sem).wait()
    sent = ready.at[pl.ds(0, peers - 1)]
    pltpu.make_async_copy(sent, sent, send_sem).wait()

    lane = lax.broadcasted_iota(jnp.int32, (1, 128), 1)

    def side(slot):
        quarter, spot = plan[16 + slot], plan[20 + slot]
        value = landed[quarter, :, spot].astype(jnp.float32)
        board[...] = value.reshape(512, 128)
        return [[board[pl.ds(2 * g + part, 64, stride=8), :] for g in range(4)] for part in range(2)]

    for b in range(2):
        left = side(2 * b)
        lefts = []
        for channel in range(8):
            keep = (lax.div(lane, 16) == channel).astype(jnp.float32)
            lefts.append(
                jnp.concatenate([(v * keep).astype(jnp.bfloat16) for v in left[0] + left[1]], axis=1)
            )
        left = jnp.concatenate(lefts, axis=0)
        right = side(2 * b + 1)
        upper = jnp.concatenate(right[0] + right[1], axis=1)
        lower = jnp.concatenate([-v for v in right[1]] + right[0], axis=1)
        right = jnp.concatenate([upper, lower], axis=0).astype(jnp.bfloat16)
        value = lax.dot_general(
            left, right, (((1,), (1,)), ((), ())), preferred_element_type=jnp.float32
        )
        result[:, b] = (value * (1.0 / FRAMES)).reshape(8, BLOCK, 2 * BLOCK)


def vmem():
    return pl.BlockSpec(memory_space=pltpu.VMEM)


def smem():
    return pl.BlockSpec(memory_space=pltpu.SMEM)


def front(volts, flags):
    bf16 = jnp.bfloat16
    cosine, sine = twiddle_tables()
    return pl.pallas_call(
        front_kernel,
        out_shape=jax.ShapeDtypeStruct((2, NX, NC, NY, 4, 2, NZ, 128), bf16),
        in_specs=[vmem()] * 7,
        out_specs=vmem(),
        scratch_shapes=[
            pltpu.VMEM((2, 2, LOCAL + FRAMES, 16, INNER), bf16),
            pltpu.VMEM((NY, 16, 128), bf16),
            pltpu.VMEM((FRAMES, 2, 16, INNER), bf16),
            pltpu.VMEM((2, NX, NC, NY, 4, 2, NZ, 128), bf16),
            pltpu.SemaphoreType.DMA((2, 3)),
            pltpu.SemaphoreType.DMA((2, 3)),
            pltpu.SemaphoreType.DMA((3,)),
            pltpu.SemaphoreType.DMA((3,)),
            pltpu.SemaphoreType.DMA((2, 7)),
            pltpu.SemaphoreType.DMA((2, 7)),
            pltpu.SemaphoreType.DMA((5,)),
        ],
        compiler_params=pltpu.CompilerParams(
            collective_id=0, has_side_effects=True, vmem_limit_bytes=40 << 20
        ),
        name="front",
    )(
        volts, flags, jnp.asarray(window_table()), jnp.asarray(first_table()),
        jnp.asarray(cosine), jnp.asarray(sine), jnp.asarray(second_table()),
    )


def back(count, plan, turned):
    bf16 = jnp.bfloat16
    return pl.pallas_call(
        functools.partial(back_kernel, count),
        out_shape=jax.ShapeDtypeStruct((8, 2, BLOCK, 2 * BLOCK), jnp.float32),
        in_specs=[smem(), vmem()],
        out_specs=vmem(),
        scratch_shapes=[
            pltpu.VMEM((512, 128), jnp.float32),
            pltpu.VMEM((NZ * NY, count, NC, 16, 128), bf16),
            pltpu.VMEM((4, 4, count, NC, NY, 16, 128), bf16),
            pltpu.SemaphoreType.DMA,
            pltpu.SemaphoreType.DMA,
        ],
        compiler_params=pltpu.CompilerParams(
            collective_id=count, has_side_effects=True, vmem_limit_bytes=40 << 20
        ),
        name="back",
    )(plan, turned)


def local(voltages, flags, pairs):
    plan = pl.pallas_call(
        plan_kernel,
        out_shape=jax.ShapeDtypeStruct((32,), jnp.int32),
        in_specs=[smem()],
        out_specs=smem(),
        name="plan",
    )(pairs)
    volts = voltages.reshape(2, 8, LOCAL, 16, INNER).transpose(1, 0, 2, 3, 4)
    live = jnp.tile(flags.astype(jnp.bfloat16), (1, 8))
    live = jnp.broadcast_to(live[:, None, :], (NY, 16, 128))
    turned = front(volts, live)
    return lax.switch(plan[24], [functools.partial(back, m) for m in range(1, 5)], plan, turned)


def solution(mesh):
    placed = (P(None, "chan", "tm"), P("chan", "tm"), P())
    return jax.shard_map(
        local,
        mesh=mesh,
        in_specs=placed,
        out_specs=P(("chan", "tm"), None, None, None),
        check_vma=False,
    )
```

time: 326 us -> 122 us (0.37)
  waiting for transfers between devices: 166 us -> 0 us
  Pallas kernels: 0 us -> 116 us
  local copies, waits for them, and re-layouts: 95.8 us -> 4.61 us
  starting transfers between devices: 28 us -> 0 us
  other arithmetic: 13.8 us -> 0.01 us
  between operations: 13.6 us -> 0.75 us
  matrix products: 4.99 us -> 0 us
    pallas_call x0 -> x3, Pallas kernels: none -> 116 us  [the longest x1 65 us: back(): pl.pallas_call(functools.partial(back_kernel, count), out_shape=jax.Shape...]
    all_to_all x1 -> x0, waiting for transfers between devices: 99.1 us -> none  [local(): lax.all_to_all(spectra, 'chan', split_axis=0, concat_axis=3, tiled=True)]
    ppermute x1 -> x0, waiting for transfers between devices: 34.5 us -> none  [shifted(): return lax.ppermute(x, axis, pairs)]
    unnamed x9 -> x14, local copies, waits for them, and re-layouts: 38.2 us -> 3.72 us
    reduce_scatter x1 -> x0, waiting for transfers between devices: 32.1 us -> none  [local(): lax.psum_scatter(partial_value, 'tm', scatter_dimension=0, tiled=True)]
    reshape x1, local copies, waits for them, and re-layouts: 24.3 us -> 0.2 us  [local(): volts = voltages.reshape(2, 8, LOCAL, 16, INNER).transpose(1, 0, 2, 3, 4)]
    all_to_all x1 -> x0, starting transfers between devices: 23.8 us -> none  [local(): lax.all_to_all(spectra, 'chan', split_axis=0, concat_axis=3, tiled=True)]
    all_to_all x1 -> x0, local copies, waits for them, and re-layouts: 22.1 us -> none  [local(): lax.all_to_all(spectra, 'chan', split_axis=0, concat_axis=3, tiled=True)]
  transfers between devices with their start and end apart: 3 -> 0, of which waited for: 3 -> 0; matrix products, arithmetic and copies ran while one was open for 1% -> 0% of each run, Pallas kernels for 0% -> 0%
where the time goes in v1:
time: 122 us
  Pallas kernels  116 us (95%)
  local copies, waits for them, and re-layouts  4.61 us (4%)
    pallas_call x1, Pallas kernels, back(): pl.pallas_call(functools.partial(back_kernel, count), out_shape=jax.Shape...  65 us
    pallas_call x1, Pallas kernels, front(): pl.pallas_call(front_kernel, out_shape=jax.ShapeDtypeStruct((2, NX, NC, N...  49.9 us
    unnamed x14, local copies, waits for them, and re-layouts  3.72 us

profile of v1, /device:TPU:1, one launch (start us, length us, event | category | flops | bytes accessed | tf_op | source)
XLA Modules:
  0.0 121.6 jit_solution(1705586570958589905)
XLA Ops:
  0.0 1.4 %plan.1 = s32[32]{0:T(128)S(1)} custom-call(s32[2,2]{1,0:T(2,128)} %pairs_ref.1), custom_call_target="tpu_custom_call" | custom-call | tf_op jit(solution)/shard_map/plan/pallas_call | solution.py:371
  1.4 2.1 %copy.15 = bf16[2,8,256,256]{3,2,1,0:T(8,128)(2,1)S(1)} copy(bf16[2,8,256,256]{3,1,2,0:T(8,128)(2,1)} %bitcast.10) | data formatting | bytes 4194304
  3.4 0.0 copy-start.5
  3.4 0.0 copy-start
  3.5 0.0 copy-start.1
  3.5 0.0 copy-start.2
  3.5 0.0 copy-start.3
  3.5 0.0 copy-start.4
  3.5 0.2 copy.17
  3.7 0.4 copy-done.5
  4.1 0.1 tile.9
  4.2 0.3 copy-done
  4.5 0.1 copy-done.1
  4.6 0.0 copy-done.2
  4.6 0.0 copy-done.3
  4.6 0.0 copy-done.4
  4.7 49.9 %front.1 = bf16[2,4,2,4,4,2,16,128]{7,6,5,4,3,2,1,0:T(8,128)(2,1)S(1)} custom-call(bf16[8,2,16,16,256]{4,3,2,1,0:T(8,128)(2,1)S(1)} %bitcast.8, bf16[4,16,128]{2,1,0:T(8,128)(2,1)S(1)} %broadcast_in_dim.2.flags, f32[16,16,256]{2,1,0:T(8,128)S(1)} %copy-done.1, bf16[256,256]{1,0:T(8,128)(2,1)S(1)} %copy-done.2, f32[128,256]{1,0:T(8,128)S(1)} %copy-done.3, ...), custom_call_target="tpu_custom_call" | custom-call | tf_op jit(solution)/shard_map/front/pallas_call | solution.py:321
  54.6 0.6 slice.3
  55.8 65.0 %conditional.1 = (f32[8,2,64,128]{3,2,1,0:T(8,128)S(1)}) conditional(s32[]{:T(128)} %bitcast, (s32[32]{0:T(128)S(1)}, bf16[2,4,2,4,4,2,16,128]{7,6,5,4,3,2,1,0:T(8,128)(2,1)S(1)}) %tuple.17, (s32[32]{0:T(128)S(1)}, bf16[2,4,2,4,4,2,16,128]{7,6,5,4,3,2,1,0:T(8,128)(2,1)S(1)}) %tuple.17, (s32[32]{0:T(128)S(1)}, ...), branch_computations={%region_0.0_spmd, %region_1.0_spmd, %region_2.0_spmd, %region_3.0_... | conditional | bytes 8 | solution.py:382
  55.8 65.0 %back.5 = f32[8,2,64,128]{3,2,1,0:T(8,128)S(1)} custom-call(s32[32]{0:T(128)S(1)} %get-tuple-element.28.plan, bf16[2,4,2,4,4,2,16,128]{7,6,5,4,3,2,1,0:T(8,128)(2,1)S(1)} %get-tuple-element.29.turned), custom_call_target="tpu_custom_call" | custom-call | tf_op jit(solution)/shard_map/cond/branch_1_fun/back/pallas_call | solution.py:351
  120.8 0.8 copy.23
  (3 shorter events, 0.0 us)
Async XLA Ops:
  3.4 0.7 copy-start.5
  3.4 1.0 copy-start
  3.5 1.1 copy-start.1
  3.5 1.1 copy-start.2
  3.5 1.2 copy-start.3
  3.5 1.2 copy-start.4

commit v2 on v1

v2 whole, which is shorter than its diff:
```python
import functools
import math

import jax
import jax.numpy as jnp
import ml_dtypes
import numpy as np
from jax import lax
from jax.experimental import pallas as pl
from jax.experimental.pallas import tpu as pltpu
from jax.sharding import PartitionSpec as P

CHANNELS = 4096
TAPS = 16
BLOCK = 64
NX, NZ, NC, NY = 4, 16, 2, 4
LOCAL = 16
FRAMES = 64
INNER = 256
MESH = pl.DeviceIdType.MESH


def window_table():
    length = TAPS * CHANNELS
    index = np.arange(length, dtype=np.float64)
    offset = (index - length / 2 + 0.5) / CHANNELS
    taper = 0.5 - 0.5 * np.cos(2.0 * math.pi * (index + 0.5) / length)
    return (np.sinc(offset) * taper).astype(np.float32).reshape(TAPS, 16, INNER)


def dft_table(order, factor):
    counts = np.arange(order)
    angle = (counts[:, None] * counts[None, :] % order).astype(np.float64) * (2.0 * math.pi / order)
    cosine = np.cos(angle) * factor
    sine = np.sin(angle) * factor
    upper = np.stack([cosine, -sine], axis=1)
    lower = np.stack([sine, cosine], axis=1)
    table = np.stack([upper, lower], axis=0)
    return table.astype(np.float32).astype(ml_dtypes.bfloat16)


def first_table():
    first = dft_table(16, 0.25).astype(np.float32)
    table = np.zeros((2, 16, 8, 8, 2, 16), np.float32)
    for f in range(8):
        table[:, :, f, f] = first.transpose(2, 3, 0, 1)
    return table.reshape(256, 256).astype(ml_dtypes.bfloat16)


def twiddle_tables():
    angle = np.arange(16)[:, None] * np.arange(INNER)[None, :] * (2.0 * math.pi / CHANNELS)
    angle = np.repeat(angle, 8, axis=0)
    return np.cos(angle).astype(np.float32), np.sin(angle).astype(np.float32)


def second_table():
    second = dft_table(INNER, 1.0 / math.sqrt(INNER))
    second = second.transpose(3, 2, 0, 1).reshape(NX, NZ, NC, 2, 2, 2 * INNER)
    return np.ascontiguousarray(second.transpose(0, 2, 3, 4, 1, 5)).reshape(2 * INNER, 2 * INNER)


def place():
    chan = lax.axis_index("chan")
    return (
        lax.div(chan, NZ * NC),
        lax.rem(lax.div(chan, NC), NZ),
        lax.rem(chan, NC),
        lax.axis_index("tm"),
    )


def device(x, z, c, y):
    return ((x * NZ + z) * NC + c, y)


def plan_kernel(pairs_ref, plan_ref, rounds_ref):
    zero, one = jnp.int32(0), jnp.int32(1)
    block = [pairs_ref[s // 2, s % 2] for s in range(4)]
    across = [lax.div(b, 4) for b in block]
    quarter = [lax.rem(b, 4) for b in block]
    fresh, order = [], []
    for s in range(4):
        new, spot = one, zero
        for e in range(s):
            spot = spot + jnp.where(quarter[e] == quarter[s], fresh[e], zero)
        for e in range(s):
            same = block[e] == block[s]
            spot = jnp.where(same, order[e], spot)
            new = jnp.where(same, zero, new)
        fresh.append(new)
        order.append(spot)
    most = zero
    for q in range(4):
        count = zero
        for s in range(4):
            count = count + jnp.where(quarter[s] == q, fresh[s], zero)
        most = jnp.maximum(most, count)
        for m in range(4):
            pick = zero
            for s in range(4):
                hit = (quarter[s] == q) & (order[s] == m)
                pick = jnp.where(hit, across[s], pick)
            plan_ref[4 * q + m] = pick
    for s in range(4):
        plan_ref[16 + s] = quarter[s]
        plan_ref[20 + s] = order[s]
    rounds_ref[0] = most - 1


def whole_kernel(
    count, plan, volts_in, flags, window_in, first_in, cosine_in, sine_in, second_in,
    result,
    volts, window, first, cosine, sine, second,
    stage, line, live, marks, filtered, spectra,
    t0, t1, t2, t3, t4, t5, t6, t7,
    board, pairing, ready, landed_a, landed_b,
    in_sem, f_send, f_recv, y_send, y_recv, x_send, x_recv, z_send, z_recv,
):
    turned = ((t0, t1, t2, t3), (t4, t5, t6, t7))
    landed = (landed_a, landed_b)
    x, z, c, y = place()
    zh, zl = lax.div(z, 4), lax.rem(z, 4)
    peers = NZ * NY

    loads = [
        pltpu.make_async_copy(source, target, in_sem.at[i])
        for i, (source, target) in enumerate(
            [
                (volts_in, volts), (window_in, window), (first_in, first),
                (cosine_in, cosine), (sine_in, sine), (second_in, second),
            ]
        )
    ]
    for load in loads:
        load.start()

    barrier = pltpu.get_barrier_semaphore()
    y_peers = [lax.rem(y + d, NY) for d in (1, 3, 2)]
    x_peers = [
        (lax.rem(x + dx, NX), lax.rem(c + dc, NC))
        for dx in (2, 1, 3, 0)
        for dc in (0, 1)
        if dx + dc > 0
    ]

    def greet(step, _):
        oz = lax.rem(z + lax.div(step, NY), NZ)
        oy = lax.rem(y + lax.rem(step, NY), NY)
        pl.semaphore_signal(barrier, inc=1, device_id=device(x, oz, c, oy), device_id_type=MESH)
        return 0

    lax.fori_loop(1, peers, greet, 0)
    for ox, oc in x_peers:
        pl.semaphore_signal(barrier, inc=1, device_id=device(ox, z, oc, y), device_id_type=MESH)

    lanes_of = lax.broadcasted_iota(jnp.int32, (LOCAL, 128), 1)
    frame_of = lax.broadcasted_iota(jnp.int32, (LOCAL, 128), 0)
    spread = (lax.rem(lanes_of, LOCAL) == frame_of).astype(jnp.float32)
    kept = jnp.dot(flags[...].astype(jnp.float32), spread, preferred_element_type=jnp.float32)
    for i in range(NY):
        live[i] = jnp.broadcast_to(kept[i : i + 1], (16, 128)).astype(jnp.bfloat16)
    line[:, :, 0:LOCAL] = jnp.zeros((2, 2, LOCAL, 16, INNER), jnp.bfloat16)
    loads[0].wait()

    def unpick(step, _):
        p, g = lax.div(step, LOCAL), lax.rem(step, LOCAL)
        start = pl.multiple_of(g * CHANNELS, CHANNELS)
        pieces = [volts[p, :, pl.ds(start + a * INNER, INNER)] for a in range(16)]
        frame = jnp.swapaxes(jnp.stack(pieces, axis=0), 0, 1)
        for i in range(8):
            stage[i, p, g] = frame[i]
        return 0

    lax.fori_loop(0, 2 * LOCAL, unpick, 0)
    pl.semaphore_wait(barrier, peers - 1 + len(x_peers))

    here = pl.ds(LOCAL + LOCAL * y, LOCAL)
    for other in y_peers:
        pltpu.make_async_remote_copy(
            src_ref=live.at[other], dst_ref=marks.at[y], send_sem=f_send, recv_sem=f_recv,
            device_id=device(x, z, c, other), device_id_type=MESH,
        ).start()
    pltpu.make_async_copy(live.at[y], marks.at[y], f_recv).start()

    def share(j):
        for p in range(2):
            for other in y_peers:
                pltpu.make_async_remote_copy(
                    src_ref=stage.at[2 * other + j, p], dst_ref=line.at[j, p, here],
                    send_sem=y_send, recv_sem=y_recv.at[2 * j + p],
                    device_id=device(x, z, c, other), device_id_type=MESH,
                ).start()
            pltpu.make_async_copy(
                stage.at[2 * y + j, p], line.at[j, p, here], y_recv.at[2 * j + p]
            ).start()

    def sift(j, p, begin, groups):
        for half in range(2):
            lanes = slice(128 * half, 128 * half + 128)

            def step(index, _):
                base = begin + index * 8
                taps = [window[t, :, lanes] for t in range(TAPS)]
                total = [None] * 8
                for u in range(8 + TAPS - 1):
                    value = line[j, p, base + 1 + u, :, lanes].astype(jnp.float32)
                    for g in range(8):
                        t = u - g
                        if 0 <= t < TAPS:
                            term = taps[t] * value
                            total[g] = term if t == 0 else total[g] + term
                for g in range(8):
                    filtered[base + g, p, :, lanes] = total[g].astype(jnp.bfloat16)
                return 0

            lax.fori_loop(0, groups, step, 0)

    def transform(part, j):
        reals, imags = [], []
        for half in range(2):
            block = filtered[pl.ds(part * LOCAL + 8 * half, 8)].reshape(256, INNER)
            value = jnp.dot(first[...], block, preferred_element_type=jnp.float32)
            real, imag = value[:128], value[128:]
            rot_real = real * cosine[...] + imag * sine[...]
            rot_imag = imag * cosine[...] - real * sine[...]
            reals.append(rot_real.reshape(16, 8, INNER))
            imags.append(rot_imag.reshape(16, 8, INNER))
        real = jnp.concatenate(reals, axis=1).reshape(256, INNER)
        imag = jnp.concatenate(imags, axis=1).reshape(256, INNER)
        rotated = jnp.concatenate([real, imag], axis=1).astype(jnp.bfloat16)
        out = lax.dot_general(
            second[...], rotated, (((1,), (1,)), ((), ())), preferred_element_type=jnp.float32
        )
        keep = marks[part][0:1].astype(jnp.float32)
        out = out * jnp.concatenate([keep, keep], axis=1)
        out = out.astype(jnp.bfloat16).reshape(NX * NC, 2, 2, NZ, 256)
        for yy in range(NY):
            low = 128 * (yy % 2)
            spectra[pl.ds((4 * j + yy) * 8, 8), part] = out[:, yy // 2, :, :, low : low + 128]

    def wait(ref, sem):
        pltpu.make_async_copy(ref, ref, sem).wait()

    def arrived(j, p):
        wait(line.at[j, p, pl.ds(LOCAL, FRAMES)], y_recv.at[2 * j + p])

    def produce(j):
        def step(part, _):
            sift(j, 1, part * LOCAL, 2)
            transform(part, j)
            return 0

        lax.fori_loop(0, 4, step, 0)

    def cross(j, dy):
        base = (4 * j + lax.rem(y + dy, NY)) * 8
        for ox, oc in x_peers:
            pltpu.make_async_remote_copy(
                src_ref=spectra.at[base + 2 * ox + oc], dst_ref=turned[j][dy].at[x, c],
                send_sem=x_send, recv_sem=x_recv.at[4 * j + dy],
                device_id=device(ox, z, oc, y), device_id_type=MESH,
            ).start()
        pltpu.make_async_copy(
            spectra.at[base + 2 * x + c], turned[j][dy].at[x, c], x_recv.at[4 * j + dy]
        ).start()

    def forward(j, dy):
        oy = lax.rem(y + dy, NY)
        wait(turned[j][dy], x_recv.at[4 * j + dy])
        if dy < 2:
            cross(j, dy + 2)
        for m in range(count):
            which = plan[zh * 4 + m]
            piece = turned[j][dy][which].astype(jnp.float32)
            board[m] = piece.reshape(256, 128)
            for oz in range(NZ):
                rows = board[m, pl.ds(oz, 16, stride=16), :]
                ready[j, oz * NY + oy, m] = rows.astype(jnp.bfloat16)

        def send(step, _):
            far = 8 - lax.div(step + 1, 2)
            oz = lax.rem(z + NZ + (2 * lax.rem(step, 2) - 1) * far, NZ)
            pltpu.make_async_remote_copy(
                src_ref=ready.at[j, oz * NY + oy], dst_ref=landed[j].at[zh, zl, :, y],
                send_sem=z_send, recv_sem=z_recv.at[j],
                device_id=device(x, oz, c, oy), device_id_type=MESH,
            ).start()
            return 0

        lax.fori_loop(0, NZ - 1, send, 0)
        source, target = ready.at[j, z * NY + oy], landed[j].at[zh, zl, :, y]
        if dy == 0:
            pltpu.make_async_copy(source, target, z_recv.at[j]).start()
        else:
            pltpu.make_async_remote_copy(
                src_ref=source, dst_ref=target, send_sem=z_send, recv_sem=z_recv.at[j],
                device_id=device(x, z, c, oy), device_id_type=MESH,
            ).start()

    share(0)
    for load in loads[1:]:
        load.wait()
    for j in range(2):
        arrived(j, 0)
        if j == 0:
            share(1)
        sift(j, 0, 0, 8)
        arrived(j, 1)
        if j == 0:
            wait(marks, f_recv)
        produce(j)
        cross(j, 0)
        cross(j, 1)
        if j == 0:
            forward(0, 0)
            forward(0, 1)
    forward(0, 2)
    forward(0, 3)
    for dy in range(NY):
        forward(1, dy)

    wait(live.at[pl.ds(0, 3)], f_send)
    wait(stage.at[pl.ds(0, 6)], y_send)
    wait(spectra.at[pl.ds(0, 56)], x_send)

    for j in range(2):
        wait(landed[j], z_recv.at[j])
        for slot in range(4):
            quarter, spot = plan[16 + slot], plan[20 + slot]
            value = landed[j][quarter, :, spot].astype(jnp.float32)
            for i in range(4):
                for core in range(NC):
                    for t in range(NY):
                        row = ((i * NC + core) * NY + t) * 2 + j
                        pairing[slot, pl.ds(8 * row, 8), :] = value[i, t, 8 * core : 8 * core + 8]

    lane = lax.broadcasted_iota(jnp.int32, (1, 128), 1)

    def side(slot):
        return [
            [pairing[slot, pl.ds(2 * g + part, 64, stride=8), :] for g in range(4)]
            for part in range(2)
        ]

    for b in range(2):
        left = side(2 * b)
        lefts = []
        for channel in range(8):
            keep = (lax.div(lane, 16) == channel).astype(jnp.float32)
            lefts.append(
                jnp.concatenate([(v * keep).astype(jnp.bfloat16) for v in left[0] + left[1]], axis=1)
            )
        left = jnp.concatenate(lefts, axis=0)
        right = side(2 * b + 1)
        upper = jnp.concatenate(right[0] + right[1], axis=1)
        lower = jnp.concatenate([-v for v in right[1]] + right[0], axis=1)
        right = jnp.concatenate([upper, lower], axis=0).astype(jnp.bfloat16)
        value = lax.dot_general(
            left, right, (((1,), (1,)), ((), ())), preferred_element_type=jnp.float32
        )
        result[:, b] = (value * (1.0 / FRAMES)).reshape(8, BLOCK, 2 * BLOCK)

    sent = ready.at[:, pl.ds(0, peers - 1)]
    wait(sent, z_send)


def vmem():
    return pl.BlockSpec(memory_space=pltpu.VMEM)


def smem():
    return pl.BlockSpec(memory_space=pltpu.SMEM)


def far():
    return pl.BlockSpec(memory_space=pl.ANY)


def whole(count, plan, volts, flags):
    bf16, f32 = jnp.bfloat16, jnp.float32
    cosine, sine = twiddle_tables()
    return pl.pallas_call(
        functools.partial(whole_kernel, count),
        out_shape=jax.ShapeDtypeStruct((8, 2, BLOCK, 2 * BLOCK), f32),
        in_specs=[smem(), far(), vmem()] + [far()] * 5,
        out_specs=vmem(),
        scratch_shapes=[
            pltpu.VMEM((2, 8, LOCAL * CHANNELS), bf16),
            pltpu.VMEM((TAPS, 16, INNER), f32),
            pltpu.VMEM((256, 256), bf16),
            pltpu.VMEM((128, INNER), f32),
            pltpu.VMEM((128, INNER), f32),
            pltpu.VMEM((512, 512), bf16),
            pltpu.VMEM((8, 2, LOCAL, 16, INNER), bf16),
            pltpu.VMEM((2, 2, LOCAL + FRAMES, 16, INNER), bf16),
            pltpu.VMEM((NY, 16, 128), bf16),
            pltpu.VMEM((NY, 16, 128), bf16),
            pltpu.VMEM((FRAMES, 2, 16, INNER), bf16),
            pltpu.VMEM((64, 4, 2, NZ, 128), bf16),
        ]
        + [pltpu.VMEM((NX, NC, 4, 2, NZ, 128), bf16)] * 8
        + [
            pltpu.VMEM((count, 256, 128), f32),
            pltpu.VMEM((4, 512, 128), f32),
            pltpu.VMEM((2, NZ * NY, count, 16, 128), bf16),
            pltpu.VMEM((4, 4, count, NY, 16, 128), bf16),
            pltpu.VMEM((4, 4, count, NY, 16, 128), bf16),
            pltpu.SemaphoreType.DMA((6,)),
            pltpu.SemaphoreType.DMA,
            pltpu.SemaphoreType.DMA,
            pltpu.SemaphoreType.DMA,
            pltpu.SemaphoreType.DMA((4,)),
            pltpu.SemaphoreType.DMA,
            pltpu.SemaphoreType.DMA((8,)),
            pltpu.SemaphoreType.DMA,
            pltpu.SemaphoreType.DMA((2,)),
        ],
        compiler_params=pltpu.CompilerParams(
            collective_id=count - 1, has_side_effects=True, vmem_limit_bytes=44 << 20
        ),
        name="whole",
    )(
        plan, volts, flags, jnp.asarray(window_table()), jnp.asarray(first_table()),
        jnp.asarray(cosine), jnp.asarray(sine), jnp.asarray(second_table()),
    )


def local(voltages, flags, pairs):
    plan, rounds = pl.pallas_call(
        plan_kernel,
        out_shape=(
            jax.ShapeDtypeStruct((24,), jnp.int32),
            jax.ShapeDtypeStruct((1,), jnp.int32),
        ),
        in_specs=[smem()],
        out_specs=(smem(), smem()),
        name="plan",
    )(pairs)
    branches = [functools.partial(whole, m) for m in range(1, 5)]
    return lax.switch(rounds[0], branches, plan, voltages, flags)


def solution(mesh):
    placed = (P(None, "chan", "tm"), P("chan", "tm"), P())
    return jax.shard_map(
        local,
        mesh=mesh,
        in_specs=placed,
        out_specs=P(("chan", "tm"), None, None, None),
        check_vma=False,
    )
```

time: 122 us -> 93.7 us (0.77)
  Pallas kernels: 116 us -> 91.7 us
  local copies, waits for them, and re-layouts: 4.61 us -> 0.8 us
    pallas_call x3 -> x2, Pallas kernels: 116 us -> 91.7 us  [the longest x1 90.3 us: whole(): pl.pallas_call(functools.partial(whole_kernel, count), out_shape=jax.Shap...]
    unnamed x14 -> x1, local copies, waits for them, and re-layouts: 3.72 us -> 0.8 us
where the time goes in v2:
time: 93.7 us; the launch traced here: 93.4 us
  Pallas kernels  91.7 us (98%)
    pallas_call x1, Pallas kernels, whole(): pl.pallas_call(functools.partial(whole_kernel, count), out_shape=jax.Shap...  90.3 us

profile of v2, /device:TPU:1, one launch (start us, length us, event | category | flops | bytes accessed | tf_op | source)
XLA Modules:
  0.0 93.4 jit_solution(13520859583059257327)
XLA Ops:
  0.0 1.4 %plan.1 = (s32[24]{0:T(128)S(1)}, s32[1]{0:T(128)}) custom-call(s32[2,2]{1,0:T(2,128)} %pairs_ref.1), custom_call_target="tpu_custom_call" | custom-call | tf_op jit(solution)/shard_map/plan/pallas_call | solution.py:429
  2.0 90.6 %conditional.1 = (f32[8,2,64,128]{3,2,1,0:T(8,128)S(1)}) conditional(s32[]{:T(128)} %bitcast, (s32[24]{0:T(128)S(1)}, bf16[2,8,65536]{2,1,0:T(8,128)(2,1)}, s32[4,16]{1,0:T(4,128)}, f32[16,16,256]{2,1,0:T(8,128)}, bf16[256,256]{1,0:T(8,128)(2,1)}, /*index=5*/f32[128,256]{1,0:T(8,128)}, f32[128,256]{1,0:T(8,128)}, ...), branch_computations={%region_0.0_spmd, %region_1.0_spmd, %region_2.0_spmd, %region_3.0_... | conditional | bytes 8 | solution.py:440
  2.0 90.3 %whole.5 = f32[8,2,64,128]{3,2,1,0:T(8,128)S(1)} custom-call(s32[24]{0:T(128)S(1)} %get-tuple-element.82.plan, bf16[2,8,65536]{2,1,0:T(8,128)(2,1)} %get-tuple-element.83.volts_in, s32[4,16]{1,0:T(4,128)} %get-tuple-element.84.flags, f32[16,16,256]{2,1,0:T(8,128)} %get-tuple-element.85.window_in, bf16[256,256]{1,0:T(8,128)(2,1)} %get-tuple-element.86.first_in, ...), custom_call_target="tpu_custom_call" | custom-call | tf_op jit(solution)/shard_map/cond/branch_1_fun/whole/pallas_call | solution.py:382
  92.6 0.8 copy.33
